TPU v7x, 256 devices: a whole 4x4x8 slice. The times are simulated.
256 devices in a mesh: row: 8 (over y, core), col: 32 (over z, x).
Axes of the slice: x: 4, y: 4, z: 8, core: 2. Of those that a mesh axis runs over, the one named last changes fastest.
Arguments:
- root_inverse: bfloat16 [8192, 8192], P('row', 'col'), may hold values from -1 to 2, as said below
- child_inverse: bfloat16 [2, 4096, 4096], P(None, 'row', 'col'), may hold values from -1 to 2, as said below
- child_panel: bfloat16 [2, 1024, 4096], P(None, 'row', 'col'), may hold values from -0.1875 to 0.1875
- ancestors: int32 [2, 8], replicated, may hold values from 0 to 63, as said below
Outputs:
- root_block: float32 [8192, 8192], P('row', 'col')
- cross_block: float32 [2, 1024, 4096], P(None, 'row', 'col')
- child_block: float32 [2, 4096, 4096], P(None, 'row', 'col')
Inputs may be any that keep to these rules, and one draw needn't show every extreme that they name: `root_inverse`: lower triangular with a positive diagonal. `child_inverse`: each child's matrix is lower triangular with a positive diagonal. `ancestors`: each row holds 8 distinct block numbers in increasing order; the first is 0 and the last 63.
All inputs are finite; a program needn't handle non-finite values.
Results may differ from a plain program's by a relative error of at most 0.0048.
Values may be sent and summed in bfloat16 or wider, within the bound.
No kernel may reach another device: no remote copies, remote signals or barrier semaphores. Data moves between devices by JAX's collectives and lax.ppermute only.
A program may use at most 192 MiB of HBM per device.

v0:
```python
import jax
import jax.numpy as jnp
from jax import lax
from jax.sharding import PartitionSpec as P

BLOCK = 128


def column_panel(shard_part):
    return lax.all_gather(shard_part, "row", axis=1, tiled=True)


def band_total(partial_value):
    return lax.psum_scatter(partial_value, "row", scatter_dimension=1, tiled=True)


def gram_reduce(left_part, right_part):
    partial_value = jnp.einsum(
        "bkm,bkn->bmn",
        lax.all_gather(left_part, "col", axis=2, tiled=True),
        right_part,
        preferred_element_type=jnp.float32,
    )
    return band_total(partial_value)


def ancestor_rows(ancestors):
    within = jnp.arange(BLOCK, dtype=jnp.int32)
    return (ancestors[:, :, None] * BLOCK + within[None, None, :]).reshape(ancestors.shape[0], -1)


def take_columns(matrix, indices):
    return jnp.take(matrix, indices, axis=1)


def shards(root_inverse, child_inverse, child_panel, ancestors):
    root_batch = root_inverse[None]
    root_block = gram_reduce(root_batch, root_batch)[0]
    band_rows, band_cols = root_block.shape
    global_rows = ancestor_rows(ancestors)
    row_local = global_rows - lax.axis_index("row") * band_rows
    row_inside = (row_local >= 0) & (row_local < band_rows)
    picked = jnp.take(root_block, jnp.clip(row_local, 0, band_rows - 1), axis=0)
    picked = jnp.where(row_inside[:, :, None], picked, 0.0)
    own_rows = band_total(picked)
    col_local = global_rows - lax.axis_index("col") * band_cols
    col_inside = (col_local >= 0) & (col_local < band_cols)
    chosen = jax.vmap(take_columns)(own_rows, jnp.clip(col_local, 0, band_cols - 1))
    chosen = jnp.where(col_inside[:, None, :], chosen, 0.0)
    ancestor_block = lax.psum(chosen.astype(jnp.bfloat16), "col")
    child_cols = column_panel(child_inverse)
    update = jnp.einsum(
        "bak,bkn->ban",
        lax.all_gather(child_panel, "col", axis=2, tiled=True),
        child_cols,
        preferred_element_type=jnp.float32,
    ).astype(jnp.bfloat16)
    update_cols = column_panel(update)
    coupled = jnp.einsum(
        "bai,bin->ban", ancestor_block, update_cols, preferred_element_type=jnp.float32
    )
    cross_block = -coupled
    coupled_half = coupled.astype(jnp.bfloat16)
    left_stack = jnp.concatenate([child_inverse, update], axis=1)
    right_stack = jnp.concatenate([child_inverse, coupled_half], axis=1)
    child_block = gram_reduce(left_stack, right_stack)
    return (root_block, cross_block, child_block)


def solution(mesh):
    in_specs = (P("row", "col"), P(None, "row", "col"), P(None, "row", "col"), P())
    out_specs = (P("row", "col"), P(None, "row", "col"), P(None, "row", "col"))
    return jax.shard_map(shards, mesh=mesh, in_specs=in_specs, out_specs=out_specs, check_vma=False)
```

profile of v0, /device:TPU:4, one launch (start us, length us, event | category | flops | bytes accessed | tf_op | source)
XLA Modules:
  0.0 697.6 jit_solution(16673732814300745927)
XLA Ops:
  7.2 0.7 all-gather.12.cloned.1.call-update
  7.9 154.6 %all-gather.12.cloned.1.call-done = bf16[1024,8192]{1,0:T(8,128)(2,1)} async-done(((bf16[1024,256]{1,0:T(8,128)(2,1)}), bf16[1024,8192]{1,0:T(8,128)(2,1)}) %all-gather.12.cloned.1.call-update) | async-done | bytes 16777232 | tf_op jit(solution)/shard_map/all_gather | solution.py:20
  162.5 13.8 %convolution_bitcast_fusion = f32[1,8192,256]{2,1,0:T(8,128)} fusion(bf16[1024,8192]{1,0:T(8,128)(2,1)} %all-gather.12.cloned.1.call-done, bf16[1024,256]{1,0:T(8,128)(2,1)} %param.4), kind=kOutput, calls=%fused_computation.2 | convolution fusion | flops 4294967296 | bytes 25690112 | tf_op jit(solution)/shard_map/bkm,bkn->bmn/dot_general | solution.py:18
  176.4 0.6 copy-done.1
  177.3 52.7 %reduce-scatter.4.cloned.1.call-done = f32[1,1024,256]{2,1,0:T(8,128)} async-done(((f32[1,8192,256]{2,1,0:T(8,128)}), f32[1,1024,256]{2,1,0:T(8,128)}) %reduce-scatter.4.cloned.1.call-update) | async-done | bytes 1048592 | tf_op jit(solution)/shard_map/reduce_scatter | solution.py:14
  229.9 7.9 %gather_fusion = f32[2048,256]{1,0:T(8,128)S(1)} fusion(f32[1024,256]{1,0:T(8,128)} %bitcast.39, s32[2048]{0:T(1024)S(1)} %bitcast_clamp_fusion), kind=kCustom, calls=%fused_computation | custom fusion | bytes 4202496 | tf_op jit(solution)/shard_map/jit(_take)/gather | solution.py:43
  237.8 1.9 copy.10
  239.7 3.4 select_select_fusion
  243.1 0.5 all-gather.8.cloned.1.call-update
  243.7 0.5 all-gather.6.cloned.1.call-update
  244.3 34.7 %reduce-scatter.6.cloned.1.call-done = f32[2,128,256]{1,2,0:T(8,128)} async-done(((f32[2,1024,256]{1,2,0:T(8,128)}), f32[2,128,256]{1,2,0:T(8,128)}) %reduce-scatter.6.cloned.1.call-update) | async-done | bytes 262160 | tf_op jit(solution)/shard_map/reduce_scatter | solution.py:14
  279.0 8.5 %gather_fusion.1 = bf16[2048,128]{1,0:T(8,128)(2,1)S(1)} fusion(f32[2,128,256]{1,2,0:T(8,128)} %reduce-scatter.6.cloned.1.call-done, s32[2048]{0:T(1024)S(1)} %bitcast.41), kind=kCustom, calls=%fused_computation.1 | custom fusion | bytes 1064960 | tf_op jit(solution)/shard_map/vmap(jit(_take))/gather | solution.py:33
  287.5 0.2 copy.11
  287.8 0.9 fusion
  288.9 18.3 %all-gather.8.cloned.1.call-done = bf16[2,4096,128]{2,1,0:T(8,128)(2,1)} async-done(((bf16[2,512,128]{2,1,0:T(8,128)(2,1)}), bf16[2,4096,128]{2,1,0:T(8,128)(2,1)}) %all-gather.8.cloned.1.call-update) | async-done | bytes 2097168 | tf_op jit(solution)/shard_map/all_gather | solution.py:10
  307.3 77.6 %all-gather.6.cloned.1.call-done = bf16[2,128,4096]{2,1,0:T(8,128)(2,1)} async-done(((bf16[2,128,128]{2,1,0:T(8,128)(2,1)}), bf16[2,128,4096]{2,1,0:T(8,128)(2,1)}) %all-gather.6.cloned.1.call-update) | async-done | bytes 2097168 | tf_op jit(solution)/shard_map/all_gather | solution.py:54
  384.9 2.9 convolution_convert_fusion
  387.9 0.8 pad_maximum_fusion
  388.7 13.6 %all_gather.18 = bf16[2,1024,128]{2,1,0:T(8,128)(2,1)S(1)} all-gather(bf16[2,128,128]{2,1,0:T(8,128)(2,1)S(1)} %convolution_convert_fusion), channel_id=1, replica_groups=mesh['row'=8,'col'=32] {'row'}, dimensions={1}, use_global_device_ids=true | all-gather | bytes 589824 | tf_op jit(solution)/shard_map/all_gather | solution.py:10
  402.4 131.4 %all-reduce.2.cloned.1.call-done = bf16[2,128,1024]{2,1,0:T(8,128)(2,1)} async-done(((bf16[2,128,1024]{2,1,0:T(8,128)(2,1)}), bf16[2,128,1024]{2,1,0:T(8,128)(2,1)}) %all-reduce.2.cloned.1.call-update) | async-done | bytes 524304 | tf_op jit(solution)/shard_map/psum | solution.py:50
  533.8 2.0 fusion.11
  535.8 106.8 %all-gather.10.cloned.1.call-done = bf16[2,640,4096]{1,2,0:T(8,128)(2,1)} async-done(((bf16[2,640,128]{1,2,0:T(8,128)(2,1)}), bf16[2,640,4096]{1,2,0:T(8,128)(2,1)}) %all-gather.10.cloned.1.call-update) | async-done | bytes 10485776 | tf_op jit(solution)/shard_map/all_gather | solution.py:20
  642.6 8.9 %fusion.1 = f32[2,4096,128]{2,1,0:T(8,128)} fusion(bf16[2,640,4096]{1,2,0:T(8,128)(2,1)} %all-gather.10.cloned.1.call-done, bf16[2,128,128]{2,1,0:T(8,128)(2,1)S(1)} %get-tuple-element.3, bf16[2,512,128]{2,1,0:T(8,128)(2,1)S(1)} %copy-done), kind=kOutput, calls=%fused_computation.8 | convolution fusion | flops 1342832640 | bytes 15007744 | tf_op jit(solution)/shard_map/bkm,bkn->bmn/dot_general | solution.py:18
  651.5 39.2 %reduce-scatter.8.cloned.1.call-done = f32[2,512,128]{2,1,0:T(8,128)} async-done(((f32[2,4096,128]{2,1,0:T(8,128)}), f32[2,512,128]{2,1,0:T(8,128)}) %reduce-scatter.8.cloned.1.call-update) | async-done | bytes 524304 | tf_op jit(solution)/shard_map/reduce_scatter | solution.py:14
  (27 shorter events, 0.9 us)
Async XLA Ops:
  7.2 155.4 %all-gather.12.cloned.1.call-start = ((), (), s32[]{:S(2)}) async-start(), calls=%async_computation.10 | async-start | bytes 17301504 | tf_op jit(solution)/shard_map/all_gather | solution.py:20
  7.9 222.0 %reduce-scatter.4.cloned.1.call-start = ((), (), s32[]{:S(2)}) async-start(), calls=%async_computation.3 | async-start | bytes 9437184 | tf_op jit(solution)/shard_map/reduce_scatter | solution.py:14
  176.3 0.7 copy-start.1
  176.3 102.7 %reduce-scatter.6.cloned.1.call-start = ((), (), s32[]{:S(2)}) async-start(), calls=%async_computation.4 | async-start | bytes 2359296 | tf_op jit(solution)/shard_map/reduce_scatter | solution.py:14
  243.1 64.2 %all-gather.8.cloned.1.call-start = ((), (), s32[]{:S(2)}) async-start(), calls=%async_computation.7 | async-start | bytes 2359296 | tf_op jit(solution)/shard_map/all_gather | solution.py:10
  243.6 141.2 %all-gather.6.cloned.1.call-start = ((), (), s32[]{:S(2)}) async-start(), calls=%async_computation.6 | async-start | bytes 2162688 | tf_op jit(solution)/shard_map/all_gather | solution.py:54
  244.2 289.6 %all-reduce.2.cloned.1.call-start = ((), (), s32[]{:S(2)}) async-start(), calls=%async_computation.5 | async-start | bytes 1048576 | tf_op jit(solution)/shard_map/psum | solution.py:50
  287.5 1.3 copy-start
  288.7 353.8 %all-gather.10.cloned.1.call-start = ((), (), s32[]{:S(2)}) async-start(), calls=%async_computation.8 | async-start | bytes 10813440 | tf_op jit(solution)/shard_map/all_gather | solution.py:20
  388.7 302.0 %reduce-scatter.8.cloned.1.call-start = ((), (), s32[]{:S(2)}) async-start(), calls=%async_computation.9 | async-start | bytes 4718592 | tf_op jit(solution)/shard_map/reduce_scatter | solution.py:14
Sparse Core Ops, SparseCore 0:
  10.5 152.0 all-gather.11
  176.5 53.4 reduce-scatter.3
  243.2 35.7 reduce-scatter.5
  280.7 26.5 all-gather.7
  309.6 75.2 all-gather.5
  388.7 145.0 all-reduce.1
  536.7 105.8 all-gather.9
  651.6 39.0 reduce-scatter.7
where the time goes:
time: 698 us
  waiting for transfers between devices  617 us (88%)
  matrix products  27.6 us (4%)
  local copies, waits for them, and re-layouts  19.5 us (3%)
  between operations  14.2 us (2%)
  blocking collectives  13.6 us (2%)
    all_gather x2, waiting for transfers between devices, gram_reduce(): lax.all_gather(left_part, 'col', axis=2, tiled=True)  261 us
    psum x1, waiting for transfers between devices, shards(): ancestor_block = lax.psum(chosen.astype(jnp.bfloat16), 'col')  131 us
    reduce_scatter x3, waiting for transfers between devices, band_total(): lax.psum_scatter(partial_value, 'row', scatter_dimension=1, tiled=True)  127 us
    all_gather x1, waiting for transfers between devices, shards(): lax.all_gather(child_panel, 'col', axis=2, tiled=True)  77.6 us
    dot_general x2, matrix products, gram_reduce(): jnp.einsum('bkm,bkn->bmn', lax.all_gather(left_part, 'col', axis=2, tiled...  22.7 us
    all_gather x1, waiting for transfers between devices, column_panel(): return lax.all_gather(shard_part, 'row', axis=1, tiled=True)  18.3 us
  transfers between devices with their start and end apart: 8, of which 8 were waited for; matrix products, arithmetic and copies ran while one was open for 2% of the time, Pallas kernels for 0%

commit v1 on v0

--- a/solution.py
+++ b/solution.py
@@ -4,6 +4,13 @@
 from jax.sharding import PartitionSpec as P
 
 BLOCK = 128
+
+
+def swapped_in(x, axis, dim):
+    size = lax.axis_size(axis)
+    parts = jnp.stack([x for _ in range(size)])
+    parts = lax.all_to_all(parts, axis, split_axis=0, concat_axis=0)
+    return jnp.concatenate(parts, axis=dim)
 
 
 def column_panel(shard_part):
@@ -17,7 +24,7 @@
 def gram_reduce(left_part, right_part):
     partial_value = jnp.einsum(
         "bkm,bkn->bmn",
-        lax.all_gather(left_part, "col", axis=2, tiled=True),
+        swapped_in(left_part, "col", 2),
         right_part,
         preferred_element_type=jnp.float32,
     )

time: 698 us -> 841 us (1.20)
  waiting for transfers between devices: 617 us -> 720 us
  local copies, waits for them, and re-layouts: 19.5 us -> 41 us
  starting transfers between devices: 0.32 us -> 20.5 us
    all_to_all x0 -> x2, waiting for transfers between devices: none -> 526 us  [swapped_in(): parts = lax.all_to_all(parts, axis, split_axis=0, concat_axis=0)]
    all_gather x2 -> x0, waiting for transfers between devices: 261 us -> none  [gram_reduce(): lax.all_gather(left_part, 'col', axis=2, tiled=True)]
    all_gather x1, waiting for transfers between devices: 77.6 us -> 0.02 us  [shards(): lax.all_gather(child_panel, 'col', axis=2, tiled=True)]
    psum x1, waiting for transfers between devices: 131 us -> 77.5 us  [shards(): ancestor_block = lax.psum(chosen.astype(jnp.bfloat16), 'col')]
    all_to_all x0 -> x2, starting transfers between devices: none -> 20.2 us  [swapped_in(): parts = lax.all_to_all(parts, axis, split_axis=0, concat_axis=0)]
    all_gather x1, waiting for transfers between devices: 18.3 us -> 0.02 us  [column_panel(): return lax.all_gather(shard_part, 'row', axis=1, tiled=True)]
    reduce_scatter x3, waiting for transfers between devices: 127 us -> 115 us  [band_total(): lax.psum_scatter(partial_value, 'row', scatter_dimension=1, tiled=True)]
    another operation x0 -> x2, local copies, waits for them, and re-layouts: none -> 11.4 us  [swapped_in(): parts = jnp.stack([x for _ in range(size)])]
  transfers between devices with their start and end apart: 8 -> 8, of which waited for: 8 -> 6; matrix products, arithmetic and copies ran while one was open for 2% -> 7% of each run, Pallas kernels for 0% -> 0%
where the time goes in v1:
time: 841 us; the launch traced here: 840 us
  waiting for transfers between devices  720 us (86%)
  local copies, waits for them, and re-layouts  41 us (5%)
  matrix products  27.3 us (3%)
  starting transfers between devices  20.5 us (2%)
  between operations  14.3 us (2%)
  blocking collectives  13.3 us (2%)
    all_to_all x2, waiting for transfers between devices, swapped_in(): parts = lax.all_to_all(parts, axis, split_axis=0, concat_axis=0)  526 us
    reduce_scatter x3, waiting for transfers between devices, band_total(): lax.psum_scatter(partial_value, 'row', scatter_dimension=1, tiled=True)  115 us
    psum x1, waiting for transfers between devices, shards(): ancestor_block = lax.psum(chosen.astype(jnp.bfloat16), 'col')  77.5 us
    dot_general x2, matrix products, gram_reduce(): jnp.einsum('bkm,bkn->bmn', swapped_in(left_part, 'col', 2), right_part, p...  22.4 us
    all_to_all x2, starting transfers between devices, swapped_in(): parts = lax.all_to_all(parts, axis, split_axis=0, concat_axis=0)  20.2 us
  transfers between devices with their start and end apart: 8, of which 6 were waited for; matrix products, arithmetic and copies ran while one was open for 7% of the time, Pallas kernels for 0%

profile of v1, /device:TPU:4, one launch (start us, length us, event | category | flops | bytes accessed | tf_op | source)
XLA Modules:
  0.0 840.4 jit_solution(173485470885616809)
XLA Ops:
  7.2 1.2 copy.13
  8.4 6.0 stack.4
  14.5 11.8 %all-to-all-start = ((bf16[32,1,1024,256]{2,3,1,0:T(8,128)(2,1)}), bf16[32,1,1024,256]{2,3,1,0:T(8,128)(2,1)}, u32[]{:S(2)}, u32[]{:S(2)}) async-start(bf16[32,1,1024,256]{2,3,1,0:T(8,128)(2,1)} %stack.4), calls=%async_computation | async-start | bytes 33554432 | tf_op jit(solution)/shard_map/all_to_all | solution.py:12
  26.3 0.7 all-gather.5.cloned.1.call-update
  27.0 0.7 all-gather.3.cloned.1.call-update
  27.8 407.5 %all-to-all-done = bf16[32,1,1024,256]{2,3,1,0:T(8,128)(2,1)} async-done(((bf16[32,1,1024,256]{2,3,1,0:T(8,128)(2,1)}), bf16[32,1,1024,256]{2,3,1,0:T(8,128)(2,1)}, u32[]{:S(2)}, u32[]{:S(2)}) %all-to-all-start) | async-done | bytes 16777248 | tf_op jit(solution)/shard_map/all_to_all | solution.py:12
  435.2 13.6 %convolution_bitcast_fusion = f32[1,8192,256]{2,1,0:T(8,128)} fusion(bf16[1024,8192]{0,1:T(8,128)(2,1)} %bitcast.2, bf16[1024,256]{1,0:T(8,128)(2,1)S(1)} %copy-done.1), kind=kOutput, calls=%fused_computation.2 | convolution fusion | flops 4294967296 | bytes 25690112 | tf_op jit(solution)/shard_map/bkm,bkn->bmn/dot_general | solution.py:25
  448.9 2.9 convolution_convert_fusion
  452.1 5.4 stack.5
  457.5 8.5 %all-to-all-start.1 = ((bf16[32,2,640,128]{2,3,1,0:T(8,128)(2,1)}), bf16[32,2,640,128]{2,3,1,0:T(8,128)(2,1)}, u32[]{:S(2)}, u32[]{:S(2)}) async-start(bf16[32,2,640,128]{2,3,1,0:T(8,128)(2,1)} %stack.5), calls=%async_computation.3 | async-start | bytes 20971520 | tf_op jit(solution)/shard_map/all_to_all | solution.py:12
  466.3 38.5 %reduce-scatter.4.cloned.1.call-done = f32[1,1024,256]{2,1,0:T(8,128)} async-done(((f32[1,8192,256]{2,1,0:T(8,128)}), f32[1,1024,256]{2,1,0:T(8,128)}) %reduce-scatter.4.cloned.1.call-update) | async-done | bytes 1048592 | tf_op jit(solution)/shard_map/reduce_scatter | solution.py:21
  504.8 7.9 gather_fusion
  512.7 1.9 copy.15
  514.6 3.4 select_select_fusion
  518.0 37.1 %reduce-scatter.6.cloned.1.call-done = f32[2,128,256]{1,2,0:T(8,128)} async-done(((f32[2,1024,256]{1,2,0:T(8,128)}), f32[2,128,256]{1,2,0:T(8,128)}) %reduce-scatter.6.cloned.1.call-update) | async-done | bytes 262160 | tf_op jit(solution)/shard_map/reduce_scatter | solution.py:21
  555.1 8.5 %gather_fusion.1 = bf16[2048,128]{1,0:T(8,128)(2,1)S(1)} fusion(f32[2,128,256]{1,2,0:T(8,128)} %reduce-scatter.6.cloned.1.call-done, s32[2048]{0:T(1024)S(1)} %bitcast.48), kind=kCustom, calls=%fused_computation.1 | custom fusion | bytes 1064960 | tf_op jit(solution)/shard_map/vmap(jit(_take))/gather | solution.py:40
  563.8 0.9 fusion
  564.8 13.3 %all_gather.11 = bf16[2,1024,128]{2,1,0:T(8,128)(2,1)S(1)} all-gather(bf16[2,128,128]{2,1,0:T(8,128)(2,1)S(1)} %convolution_convert_fusion), channel_id=1, replica_groups=mesh['row'=8,'col'=32] {'row'}, dimensions={1}, use_global_device_ids=true | all-gather | bytes 589824 | tf_op jit(solution)/shard_map/all_gather | solution.py:17
  578.1 118.6 %all-to-all-done.1 = bf16[32,2,640,128]{2,3,1,0:T(8,128)(2,1)} async-done(((bf16[32,2,640,128]{2,3,1,0:T(8,128)(2,1)}), bf16[32,2,640,128]{2,3,1,0:T(8,128)(2,1)}, u32[]{:S(2)}, u32[]{:S(2)}) %all-to-all-start.1) | async-done | bytes 10485792 | tf_op jit(solution)/shard_map/all_to_all | solution.py:12
  696.8 9.5 %copy.18 = bf16[2,640,32,128]{1,3,2,0:T(8,128)(2,1)} copy(bf16[2,640,32,128]{1,3,0,2:T(8,128)(2,1)} %bitcast.9) | data formatting | bytes 20971520 | tf_op jit(solution)/shard_map/reshape | solution.py:13
  706.3 77.5 %all-reduce.2.cloned.1.call-done = bf16[2,128,1024]{2,1,0:T(8,128)(2,1)} async-done(((bf16[2,128,1024]{2,1,0:T(8,128)(2,1)}), bf16[2,128,1024]{2,1,0:T(8,128)(2,1)}) %all-reduce.2.cloned.1.call-update) | async-done | bytes 524304 | tf_op jit(solution)/shard_map/psum | solution.py:57
  783.7 2.0 fusion.11
  785.7 8.8 %fusion.1 = f32[2,4096,128]{2,1,0:T(8,128)} fusion(bf16[2,640,4096]{1,2,0:T(8,128)(2,1)} %bitcast.49, bf16[2,128,128]{2,1,0:T(8,128)(2,1)S(1)} %get-tuple-element.3, bf16[2,512,128]{2,1,0:T(8,128)(2,1)S(1)} %copy-done), kind=kOutput, calls=%fused_computation.8 | convolution fusion | flops 1342832640 | bytes 15007744 | tf_op jit(solution)/shard_map/bkm,bkn->bmn/dot_general | solution.py:25
  794.6 38.9 %reduce-scatter.8.cloned.1.call-done = f32[2,512,128]{2,1,0:T(8,128)} async-done(((f32[2,4096,128]{2,1,0:T(8,128)}), f32[2,512,128]{2,1,0:T(8,128)}) %reduce-scatter.8.cloned.1.call-update) | async-done | bytes 524304 | tf_op jit(solution)/shard_map/reduce_scatter | solution.py:21
  (30 shorter events, 1.1 us)
Async XLA Ops:
  14.4 420.8 %copy-start.1 = (bf16[1024,256]{1,0:T(8,128)(2,1)S(1)}, bf16[1024,256]{1,0:T(8,128)(2,1)}, u32[]{:S(2)}) copy-start(bf16[1024,256]{1,0:T(8,128)(2,1)} %param.4) | copy-start | bytes 1572868
  14.5 420.8 %all-to-all-start = ((bf16[32,1,1024,256]{2,3,1,0:T(8,128)(2,1)}), bf16[32,1,1024,256]{2,3,1,0:T(8,128)(2,1)}, u32[]{:S(2)}, u32[]{:S(2)}) async-start(bf16[32,1,1024,256]{2,3,1,0:T(8,128)(2,1)} %stack.4), calls=%async_computation | async-start | bytes 33554432 | tf_op jit(solution)/shard_map/all_to_all | solution.py:12
  26.2 422.6 %all-gather.5.cloned.1.call-start = ((), (), s32[]{:S(2)}) async-start(), calls=%async_computation.9 | async-start | bytes 2359296 | tf_op jit(solution)/shard_map/all_gather | solution.py:17
  27.0 421.9 %all-gather.3.cloned.1.call-start = ((), (), s32[]{:S(2)}) async-start(), calls=%async_computation.8 | async-start | bytes 2162688 | tf_op jit(solution)/shard_map/all_gather | solution.py:61
  27.7 477.1 %reduce-scatter.4.cloned.1.call-start = ((), (), s32[]{:S(2)}) async-start(), calls=%async_computation.5 | async-start | bytes 9437184 | tf_op jit(solution)/shard_map/reduce_scatter | solution.py:21
  448.8 3.0 copy-start
  457.5 8.5 %copy-start.2 = (s32[2,8]{1,0:T(2,128)S(1)}, s32[2,8]{1,0:T(2,128)}, u32[]{:S(2)}) copy-start(s32[2,8]{1,0:T(2,128)} %param.7) | copy-start | bytes 196
  457.5 239.3 %all-to-all-start.1 = ((bf16[32,2,640,128]{2,3,1,0:T(8,128)(2,1)}), bf16[32,2,640,128]{2,3,1,0:T(8,128)(2,1)}, u32[]{:S(2)}, u32[]{:S(2)}) async-start(bf16[32,2,640,128]{2,3,1,0:T(8,128)(2,1)} %stack.5), calls=%async_computation.3 | async-start | bytes 20971520 | tf_op jit(solution)/shard_map/all_to_all | solution.py:12
  466.0 89.1 %reduce-scatter.6.cloned.1.call-start = ((), (), s32[]{:S(2)}) async-start(), calls=%async_computation.6 | async-start | bytes 2359296 | tf_op jit(solution)/shard_map/reduce_scatter | solution.py:21
  518.0 265.8 %all-reduce.2.cloned.1.call-start = ((), (), s32[]{:S(2)}) async-start(), calls=%async_computation.7 | async-start | bytes 1048576 | tf_op jit(solution)/shard_map/psum | solution.py:57
  564.8 268.7 %reduce-scatter.8.cloned.1.call-start = ((), (), s32[]{:S(2)}) async-start(), calls=%async_computation.10 | async-start | bytes 4718592 | tf_op jit(solution)/shard_map/reduce_scatter | solution.py:21
Sparse Core Ops, SparseCore 0:
  28.9 28.8 all-gather.4
  60.3 230.2 all-gather.2
  449.0 55.8 reduce-scatter.3
  518.1 36.9 reduce-scatter.5
  564.9 218.7 all-reduce.1
  794.7 38.7 reduce-scatter.7
